TPU v7x, 32 devices: a whole 2x2x4 slice. The times are simulated.
32 devices in a mesh: rep: 1, tp: 16 (over z, y, x), sub: 2 (over core).
Axes of the slice: x: 2, y: 2, z: 4, core: 2. Of those that a mesh axis runs over, the one named last changes fastest.
Arguments:
- tokens: bfloat16 [256, 8192], P(('rep', 'tp'), 'sub'), may hold values from -6 to 6
- gate_projection_weight: bfloat16 [8192, 28672], P('sub', 'tp'), may hold values from -0.0625 to 0.0625
- up_projection_weight: bfloat16 [8192, 28672], P('sub', 'tp'), may hold values from -0.0625 to 0.0625
- down_projection_weight: bfloat16 [28672, 8192], P('tp', 'sub'), may hold values from -0.03125 to 0.03125
- adapter_down_store: bfloat16 [64, 64, 8192], P('tp', None, 'sub'), may hold values from -0.0625 to 0.0625
- adapter_up_store: bfloat16 [64, 64, 8192], P('tp', None, 'sub'), may hold values from -0.75 to 0.75
- request_adapter_index: int32 [256], P('rep'), may hold values from 0 to 63, never falling along the last dimension, each value on 1 to 32 neighbouring positions
- adapter_store_row: int32 [64], replicated, may hold values from 0 to 63, each once
Outputs:
- mixed: bfloat16 [256, 8192], P(('rep', 'tp'), 'sub')
Inputs may be any that keep to these rules, and one draw needn't show every extreme that they name: `request_adapter_index`: never falling; each of the 64 adapters is named by 1 to 32 consecutive requests, one adapter by exactly 32. A permutation: the panels of adapter a are row adapter_store_row[a] of adapter_down_store and adapter_up_store.
All inputs are finite; a program needn't handle non-finite values.
Results may differ from a plain program's by a relative error of at most 0.0051.
Values may be sent and summed in bfloat16 or wider, within the bound.
A program may use at most 192 MiB of HBM per device.

v0:
```python
import jax
import jax.numpy as jnp
from jax import lax
from jax.sharding import PartitionSpec as P


def on_device(
    tokens,
    gate_projection_weight,
    up_projection_weight,
    down_projection_weight,
    adapter_down_store,
    adapter_up_store,
    request_adapter_index,
    adapter_store_row,
):
    every_row = lax.all_gather(tokens, "tp", axis=0, tiled=True)
    batch_row_count = every_row.shape[0]
    row_span = batch_row_count // 8
    local_store_rows = adapter_down_store.shape[0]
    tp_place = lax.axis_index("tp")
    numbers = jnp.arange(adapter_store_row.shape[0], dtype=jnp.int32)
    gate_part = jnp.dot(every_row, gate_projection_weight, preferred_element_type=jnp.float32)
    up_part = jnp.dot(every_row, up_projection_weight, preferred_element_type=jnp.float32)
    begins = []
    members = []
    low_list = []
    for store_row_index in range(local_store_rows):
        target = tp_place * local_store_rows + store_row_index
        adapter = jnp.sum(jnp.where(adapter_store_row == target, numbers, 0))
        offset = jnp.sum((request_adapter_index < adapter).astype(jnp.int32))
        row_begin = jnp.minimum(offset, batch_row_count - row_span)
        row_block = lax.dynamic_slice_in_dim(every_row, row_begin, row_span, 0)
        member = lax.dynamic_slice_in_dim(request_adapter_index, row_begin, row_span, 0) == adapter
        low_list.append(
            lax.dot_general(
                row_block,
                adapter_down_store[store_row_index],
                (((1,), (1,)), ((), ())),
                preferred_element_type=jnp.float32,
            )
        )
        begins.append(row_begin)
        members.append(member)
    low_parts = jnp.stack(low_list)
    gate_sum, up_sum, low_sum = lax.psum((gate_part, up_part, low_parts), "sub")
    hidden = (jax.nn.silu(gate_sum) * up_sum).astype(jnp.bfloat16)
    rank_activation = low_sum.astype(jnp.bfloat16)
    adapter_output = jnp.zeros((batch_row_count, adapter_up_store.shape[2]), jnp.float32)
    for store_row_index in range(local_store_rows):
        product = jnp.dot(
            rank_activation[store_row_index],
            adapter_up_store[store_row_index],
            preferred_element_type=jnp.float32,
        )
        product = jnp.where(members[store_row_index][:, None], product, 0.0)
        current = lax.dynamic_slice_in_dim(adapter_output, begins[store_row_index], row_span, 0)
        adapter_output = lax.dynamic_update_slice_in_dim(
            adapter_output, current + product, begins[store_row_index], 0
        )
    base_rows = jnp.dot(hidden, down_projection_weight, preferred_element_type=jnp.float32)
    summed = lax.psum_scatter(base_rows + adapter_output, "tp", scatter_dimension=0, tiled=True)
    return summed.astype(jnp.bfloat16)


def solution(mesh):
    return jax.shard_map(
        on_device,
        mesh=mesh,
        in_specs=(
            P(("rep", "tp"), "sub"),
            P("sub", "tp"),
            P("sub", "tp"),
            P("tp", "sub"),
            P("tp", None, "sub"),
            P("tp", None, "sub"),
            P("rep"),
            P(),
        ),
        out_specs=P(("rep", "tp"), "sub"),
        check_vma=False,
    )
```

profile of v0, /device:TPU:0, one launch (start us, length us, event | category | flops | bytes accessed | tf_op | source)
XLA Modules:
  0.0 247.1 jit_solution(6386295915246044087)
XLA Ops:
  6.5 0.7 all-gather.2.cloned.1.call-update
  7.3 66.3 %all-gather.2.cloned.1.call-done = bf16[256,4096]{1,0:T(8,128)(2,1)} async-done(((bf16[16,4096]{1,0:T(8,128)(2,1)}), bf16[256,4096]{1,0:T(8,128)(2,1)}) %all-gather.2.cloned.1.call-update) | async-done | bytes 2097168 | tf_op jit(solution)/shard_map/all_gather | solution.py:17
  73.6 11.2 %fusion.37 = f32[256,1792]{1,0:T(8,128)} fusion(bf16[256,4096]{1,0:T(8,128)(2,1)} %all-gather.2.cloned.1.call-done, bf16[4096,1792]{1,0:T(8,128)(2,1)} %param.9), kind=kOutput, calls=%fused_computation.64 | convolution fusion | flops 3758096384 | bytes 18612224 | tf_op jit(solution)/shard_map/dot_general | solution.py:23
  84.8 8.5 %fusion.38 = f32[256,1792]{1,0:T(8,128)} fusion(bf16[256,4096]{1,0:T(8,128)(2,1)S(1)} %copy-done.2, bf16[4096,1792]{1,0:T(8,128)(2,1)} %param.10), kind=kOutput, calls=%fused_computation.65 | convolution fusion | flops 3758096384 | bytes 18612224 | tf_op jit(solution)/shard_map/dot_general | solution.py:24
  94.0 0.7 fusion.33
  94.7 3.3 %fusion.29 = (s32[]{:T(128)}, s32[]{:T(128)}, s32[]{:T(128)}, s32[]{:T(128)}) fusion(s32[256]{0:T(256)S(1)} %copy-done.3, s32[]{:T(128)} %get-tuple-element.9, s32[]{:T(128)} %get-tuple-element.11, s32[]{:T(128)} %get-tuple-element.12, s32[]{:T(128)} %get-tuple-element.10), kind=kLoop, calls=%fused_computation.52 | loop fusion | flops 3068 | bytes 1056 | tf_op jit(solution)/shard_map/reduce_sum | solution.py:31
  100.4 2.6 %dynamic-slice_compare_fusion = (pred[32]{0:T(512)(128)(4,1)S(1)}, pred[32]{0:T(512)(128)(4,1)S(1)}, pred[32]{0:T(512)(128)(4,1)S(1)}, pred[32]{0:T(512)(128)(4,1)S(1)}) fusion(s32[256]{0:T(256)S(1)} %copy-done.3, s32[]{:T(128)S(6)} %select_n.56, s32[]{:T(128)} %get-tuple-element.11, s32[]{:T(128)} %get-tuple-element.10, s32[]{:T(128)S(6)} %select_n.50, ...), kind=kLoop, calls=%fused_computation.59 | loop fusion | flops 128 | bytes 672 | tf_op jit(solution)/shard_map/eq | solution.py:34
  103.0 1.3 convolution_bitcast_fusion
  104.3 1.2 convolution_bitcast_fusion.1
  105.5 1.2 convolution_bitcast_fusion.2
  106.8 1.3 convolution_bitcast_fusion.3
  108.1 3.6 %psum.23 = bf16[4,32,64]{2,1,0:T(8,128)(2,1)S(1)} all-reduce(f32[4,32,64]{2,1,0:T(8,128)S(1)} %pad_maximum_fusion), channel_id=1, replica_groups=mesh['rep'=1,'tp'=16,'sub'=2] {'sub'}, use_global_device_ids=true, to_apply=%region_10.11 | all-reduce | flops 8192 | bytes 49152 | tf_op jit(solution)/shard_map/psum | solution.py:46
  111.7 1.3 convolution_select_fusion.3
  113.0 2.5 broadcast_in_dim.44
  115.5 2.8 %dynamic_update_slice.12 = f32[256,4096]{1,0:T(8,128)} dynamic-update-slice(f32[256,4096]{1,0:T(8,128)} %broadcast_in_dim.44, f32[32,4096]{1,0:T(8,128)S(1)} %convolution_select_fusion.3, s32[]{:T(128)S(6)} %select_n.50, s32[]{:T(128)} %constant.7.clone.1) | dynamic-update-slice | bytes 1048580 | tf_op jit(solution)/shard_map/dynamic_update_slice | solution.py:58
  118.3 1.3 fusion.2
  119.6 2.9 %dynamic_update_slice.13 = f32[256,4096]{1,0:T(8,128)} dynamic-update-slice(f32[256,4096]{1,0:T(8,128)} %dynamic_update_slice.12, f32[32,4096]{1,0:T(8,128)S(1)} %fusion.2, s32[]{:T(128)S(6)} %select_n.52, s32[]{:T(128)} %constant.7.clone.1) | dynamic-update-slice | bytes 1048580 | tf_op jit(solution)/shard_map/dynamic_update_slice | solution.py:58
  122.5 1.3 fusion.1
  123.9 2.9 %dynamic_update_slice.14 = f32[256,4096]{1,0:T(8,128)} dynamic-update-slice(f32[256,4096]{1,0:T(8,128)} %dynamic_update_slice.13, f32[32,4096]{1,0:T(8,128)S(1)} %fusion.1, s32[]{:T(128)S(6)} %select_n.54, s32[]{:T(128)} %constant.7.clone.1) | dynamic-update-slice | bytes 1048580 | tf_op jit(solution)/shard_map/dynamic_update_slice | solution.py:58
  126.8 1.3 fusion
  128.1 2.9 %dynamic_update_slice.15 = f32[256,4096]{1,0:T(8,128)} dynamic-update-slice(f32[256,4096]{1,0:T(8,128)} %dynamic_update_slice.14, f32[32,4096]{1,0:T(8,128)S(1)} %fusion, s32[]{:T(128)S(6)} %select_n.56, s32[]{:T(128)} %constant.7.clone.1) | dynamic-update-slice | bytes 1048580 | tf_op jit(solution)/shard_map/dynamic_update_slice | solution.py:58
  131.0 13.5 %convolution_add_fusion = f32[256,4096]{1,0:T(8,128)} fusion(f32[256,4096]{1,0:T(8,128)} %dynamic_update_slice.15, bf16[1792,4096]{1,0:T(8,128)(2,1)} %param.11, f32[256,1792]{1,0:T(8,128)} %get-tuple-element.13, f32[256,1792]{1,0:T(8,128)} %get-tuple-element.14), kind=kOutput, calls=%fused_computation | convolution fusion | flops 3761897472 | bytes 26738688 | tf_op jit(solution)/shard_map/dot_general | solution.py:61
  144.5 94.4 %reduce-scatter.2.cloned.1.call-done = f32[16,4096]{1,0:T(8,128)} async-done(((f32[256,4096]{1,0:T(8,128)}), f32[16,4096]{1,0:T(8,128)}) %reduce-scatter.2.cloned.1.call-update) | async-done | bytes 262160 | tf_op jit(solution)/shard_map/reduce_scatter | solution.py:62
  239.0 1.6 convert_element_type.27
  (17 shorter events, 0.7 us)
Async XLA Ops:
  6.5 67.0 %all-gather.2.cloned.1.call-start = ((), (), s32[]{:S(2)}) async-start(), calls=%async_computation.1 | async-start | bytes 2228224 | tf_op jit(solution)/shard_map/all_gather | solution.py:17
  7.3 123.8 %all-reduce.3.cloned.1.call-start = ((), (), s32[]{:S(2)}) async-start(), calls=%async_computation.3 | async-start | bytes 7340032 | tf_op jit(solution)/shard_map/psum | solution.py:46
  73.6 11.2 %copy-start.2 = (bf16[256,4096]{1,0:T(8,128)(2,1)S(1)}, bf16[256,4096]{1,0:T(8,128)(2,1)}, u32[]{:S(2)}) copy-start(bf16[256,4096]{1,0:T(8,128)(2,1)} %all-gather.2.cloned.1.call-done) | copy-start | bytes 6291460
  93.3 0.7 copy-start.4
  93.3 1.4 copy-start.3
  93.3 9.7 %copy-start = (bf16[4,64,4096]{2,1,0:T(8,128)(2,1)S(1)}, bf16[4,64,4096]{2,1,0:T(8,128)(2,1)}, u32[]{:S(2)}) copy-start(bf16[4,64,4096]{2,1,0:T(8,128)(2,1)} %param.12) | copy-start | bytes 6291460
  93.3 145.6 %reduce-scatter.2.cloned.1.call-start = ((), (), s32[]{:S(2)}) async-start(), calls=%async_computation.2 | async-start | bytes 4456448 | tf_op jit(solution)/shard_map/reduce_scatter | solution.py:62
  113.0 5.3 %copy-start.1 = (bf16[4,64,4096]{2,1,0:T(8,128)(2,1)S(1)}, bf16[4,64,4096]{2,1,0:T(8,128)(2,1)}, u32[]{:S(2)}) copy-start(bf16[4,64,4096]{2,1,0:T(8,128)(2,1)} %param.13) | copy-start | bytes 6291460
Sparse Core Ops, SparseCore 0:
  10.1 63.3 all-gather.1
  93.5 22.9 all-reduce.2
  144.6 94.2 reduce-scatter.1
where the time goes:
time: 248 us; the launch traced here: 247 us
  waiting for transfers between devices  161 us (65%)
  matrix products  43.4 us (18%)
  between operations  15.7 us (6%)
  local copies, waits for them, and re-layouts  14.7 us (6%)
  other arithmetic  8.18 us (3%)
  blocking collectives  3.62 us (1%)
    reduce_scatter x1, waiting for transfers between devices, on_device(): lax.psum_scatter(base_rows + adapter_output, 'tp', scatter_dimension=0, t...  94.4 us
    all_gather x1, waiting for transfers between devices, on_device(): every_row = lax.all_gather(tokens, 'tp', axis=0, tiled=True)  66.3 us
    dot_general x1, matrix products, on_device(): jnp.dot(hidden, down_projection_weight, preferred_element_type=jnp.float32)  13.5 us
    dynamic_update_slice x4, local copies, waits for them, and re-layouts, on_device(): lax.dynamic_update_slice_in_dim(adapter_output, current + product, begins...  11.6 us
    dot_general x1, matrix products, on_device(): jnp.dot(every_row, gate_projection_weight, preferred_element_type=jnp.flo...  11.2 us
    dot_general x1, matrix products, on_device(): jnp.dot(every_row, up_projection_weight, preferred_element_type=jnp.float32)  8.51 us
    dot_general x4, matrix products, on_device(): jnp.dot(rank_activation[store_row_index], adapter_up_store[store_row_inde...  5.24 us
    dot_general x4, matrix products, on_device(): lax.dot_general(row_block, adapter_down_store[store_row_index], (((1,), (...  5.01 us
  transfers between devices with their start and end apart: 3, of which 2 were waited for; matrix products, arithmetic and copies ran while one was open for 12% of the time, Pallas kernels for 0%

commit v1 on v0

--- a/solution.py
+++ b/solution.py
@@ -1,10 +1,19 @@
 import jax
 import jax.numpy as jnp
 from jax import lax
+from jax.experimental import pallas as pl
+from jax.experimental.pallas import tpu as pltpu
 from jax.sharding import PartitionSpec as P
 
-
-def on_device(
+MESH = pl.DeviceIdType.MESH
+ZS = 4
+STEPS = 8
+SLOTS = 6
+PARTS = 8
+TILE = 256
+
+
+def plain(
     tokens,
     gate_projection_weight,
     up_projection_weight,
@@ -63,9 +72,367 @@
     return summed.astype(jnp.bfloat16)
 
 
+def layer_kernel(
+    tokens_ref, gate_hbm, up_hbm, down_hbm, adown_hbm, aup_hbm, index_ref, store_ref,
+    out_ref,
+    tok, wg, wu, wa, wd, acc, low, from_core, low_from_core, hid, base,
+    send1, recv1, send2, recv2, send3, recv3, index_rel,
+    w_sem, d_sem, z_send, z_recv, n_send, n_recv, e_send, e_recv, h_send, h_recv,
+    r_send, r_recv, rz_send, rz_recv,
+):
+    tp = lax.axis_index("tp")
+    sub = lax.axis_index("sub")
+    rep = lax.axis_index("rep")
+    rows = tok.shape[1]
+    own = tokens_ref.shape[0]
+    group = ZS * own
+    width = tok.shape[2]
+    tiles = acc.shape[0]
+    columns = base.shape[2]
+    half = rows // 2
+
+    x = tp % 2
+    y = (tp // 2) % 2
+    z = tp // 4
+    flips = (z, z + 1 - 2 * (z % 2), z + 2 - 4 * (z // 2), 3 - z)
+    crosses = (0, 1 - 2 * x, 2 - 4 * y, 3 - 2 * (x + 2 * y))
+
+    def place(q, k):
+        return flips[k] * 4 + x + 2 * y + crosses[q]
+
+    z_peers = [(rep, flips[k] * 4 + x + 2 * y, sub) for k in range(1, ZS)]
+    first = (rep, tp + crosses[1] * (1 - sub) + crosses[2] * sub, sub)
+    second = (rep, tp + crosses[2] * (1 - sub) + crosses[1] * sub, sub)
+    first_rows = pl.ds(pl.multiple_of((1 + sub) * group, group), group)
+    second_rows = pl.ds(pl.multiple_of((2 - sub) * group, group), group)
+    own_rows = pl.ds(0, group)
+    cross_rows = pl.ds(3 * group, group)
+    core = (rep, tp, 1 - sub)
+    my_half = pl.ds(pl.multiple_of(sub * half, half), half)
+    core_half = pl.ds(pl.multiple_of((1 - sub) * half, half), half)
+
+    def weight_copies(c):
+        slot = c % SLOTS
+        part = pl.ds(pl.multiple_of(c * width, width), width)
+        return (
+            pltpu.make_async_copy(gate_hbm.at[part, :], wg.at[slot], w_sem.at[0, slot]),
+            pltpu.make_async_copy(up_hbm.at[part, :], wu.at[slot], w_sem.at[1, slot]),
+            pltpu.make_async_copy(adown_hbm.at[:, part], wa.at[slot], w_sem.at[2, slot]),
+        )
+
+    hidden_units = down_hbm.shape[0]
+    down_copies = (
+        pltpu.make_async_copy(down_hbm, wd.at[pl.ds(0, hidden_units), :], d_sem.at[0]),
+        pltpu.make_async_copy(
+            aup_hbm, wd.at[pl.ds(hidden_units, aup_hbm.shape[0]), :], d_sem.at[1]
+        ),
+    )
+
+    def remote(source, target, sent, received, device):
+        return pltpu.make_async_remote_copy(
+            src_ref=source, dst_ref=target, send_sem=sent, recv_sem=received,
+            device_id=device, device_id_type=MESH,
+        )
+
+    def z_copy(c, k):
+        return remote(
+            tok.at[c, pl.ds(0, own), :], tok.at[c, pl.ds(k * own, own), :],
+            z_send.at[c, k - 1], z_recv.at[c, k - 1], z_peers[k - 1],
+        )
+
+    def near_copies(c):
+        return (
+            remote(tok.at[c, own_rows, :], tok.at[c, first_rows, :],
+                   n_send.at[0, c], n_recv.at[0, c], first),
+            remote(tok.at[c, own_rows, :], tok.at[c, second_rows, :],
+                   n_send.at[1, c], n_recv.at[1, c], second),
+        )
+
+    def cross_copy(c):
+        return remote(tok.at[c, first_rows, :], tok.at[c, cross_rows, :],
+                      n_send.at[2, c], n_recv.at[2, c], second)
+
+    def core_copy(j):
+        return remote(acc.at[j, core_half, :], from_core.at[j], e_send.at[j], e_recv.at[j], core)
+
+    low_copy = remote(low.at[core_half, :], low_from_core, e_send.at[tiles], e_recv.at[tiles], core)
+
+    def hidden_copy(j):
+        block = hid.at[my_half, pl.ds(pl.multiple_of(j * TILE, TILE), TILE)]
+        return remote(block, block, h_send.at[j], h_recv.at[j], core)
+
+    def sum_copy1(n):
+        return remote(send1.at[n], recv1.at[n], r_send.at[0, n], r_recv.at[0, n], second)
+
+    def sum_copy2(n):
+        return remote(send2.at[n], recv2.at[n], r_send.at[1, n], r_recv.at[1, n], first)
+
+    def sum_copy3(n, k):
+        return remote(send3.at[n, k - 1], recv3.at[n, k - 1],
+                      rz_send.at[n, k - 1], rz_recv.at[n, k - 1], z_peers[k - 1])
+
+    barrier = pltpu.get_barrier_semaphore()
+    peers = z_peers + [first, second, core]
+    for peer in peers:
+        pl.semaphore_signal(barrier, inc=1, device_id=peer, device_id_type=MESH)
+    for c in range(SLOTS):
+        for copy in weight_copies(c):
+            copy.start()
+    for copy in down_copies:
+        copy.start()
+    for c in range(STEPS):
+        tok[c, 0:own, :] = tokens_ref[:, c * width:(c + 1) * width]
+    pl.semaphore_wait(barrier, len(peers))
+    for c in range(STEPS):
+        for k in range(1, ZS):
+            z_copy(c, k).start()
+
+    @pl.loop(0, tiles)
+    def _(j):
+        acc[j] = jnp.zeros(acc.shape[1:], jnp.float32)
+
+    low[...] = jnp.zeros_like(low)
+    for q in range(4):
+        for k in range(ZS):
+            source = pl.ds(pl.multiple_of(place(q, k) * own, own), own)
+            index_rel[pl.ds(q * group + k * own, own), :] = index_ref[source, :]
+
+    def gather_step(t, carry):
+        @pl.when(t < STEPS)
+        def _():
+            for k in range(1, ZS):
+                z_copy(t, k).wait_recv()
+            for copy in near_copies(t):
+                copy.start()
+
+        @pl.when((t >= 1) & (t < STEPS + 1))
+        def _():
+            near_copies(t - 1)[0].wait_recv()
+            cross_copy(t - 1).start()
+
+        @pl.when(t >= 2)
+        def _():
+            c = t - 2
+            slot = c % SLOTS
+            near_copies(c)[1].wait_recv()
+            cross_copy(c).wait_recv()
+            for copy in weight_copies(c):
+                copy.wait()
+
+            @pl.loop(0, tiles)
+            def _(j):
+                part = pl.ds(pl.multiple_of(j * TILE, TILE), TILE)
+                acc[j, :, 0:TILE] += jnp.dot(
+                    tok[c], wg[slot, :, part], preferred_element_type=jnp.float32
+                )
+                acc[j, :, TILE:2 * TILE] += jnp.dot(
+                    tok[c], wu[slot, :, part], preferred_element_type=jnp.float32
+                )
+
+                @pl.when(c == STEPS - 1)
+                def _():
+                    core_copy(j).start()
+
+            low[...] += lax.dot_general(
+                tok[c], wa[slot], (((1,), (1,)), ((), ())), preferred_element_type=jnp.float32
+            )
+
+            @pl.when(c + SLOTS < STEPS)
+            def _():
+                for copy in weight_copies(c + SLOTS):
+                    copy.start()
+
+        return carry
+
+    lax.fori_loop(0, STEPS + 2, gather_step, 0)
+    low_copy.start()
+
+    @pl.loop(0, tiles)
+    def _(j):
+        core_copy(j).wait_recv()
+        gate = acc[j, my_half, 0:TILE] + from_core[j, :, 0:TILE]
+        up = acc[j, my_half, TILE:2 * TILE] + from_core[j, :, TILE:2 * TILE]
+        value = gate / (1.0 + jnp.exp(-gate)) * up
+        hid[my_half, pl.ds(pl.multiple_of(j * TILE, TILE), TILE)] = value.astype(jnp.bfloat16)
+        hidden_copy(j).start()
+
+    low_copy.wait_recv()
+    adapters = store_ref.shape[1]
+    ranks = low.shape[1]
+    local = ranks // 64
+    numbers = lax.broadcasted_iota(jnp.int32, (half, adapters), 1)
+    store = jnp.broadcast_to(store_ref[...].astype(jnp.float32), (half, adapters))
+    row_of = jnp.sum(
+        jnp.where(index_rel[my_half, :] == numbers, store, 0.0), axis=1, keepdims=True
+    )
+    held = lax.broadcasted_iota(jnp.int32, (half, ranks), 1) // 64 + tp * local
+    low_sum = low[my_half, :] + low_from_core[...]
+    low_sum = jnp.where(row_of == held.astype(jnp.float32), low_sum, 0.0)
+    hid[my_half, pl.ds(tiles * TILE, TILE)] = low_sum.astype(jnp.bfloat16)
+    hidden_copy(tiles).start()
+    for copy in down_copies:
+        copy.wait()
+
+    @pl.loop(0, tiles + 1)
+    def _(j):
+        hidden_copy(j).wait_recv()
+
+    def sum_step(t, carry):
+        @pl.when(t < PARTS)
+        def _():
+            @pl.loop(0, columns // TILE)
+            def _(i):
+                part = pl.ds(pl.multiple_of(i * TILE, TILE), TILE)
+                whole = pl.ds(pl.multiple_of(t * columns + i * TILE, TILE), TILE)
+                base[t, :, part] = jnp.dot(
+                    hid[...], wd[:, whole], preferred_element_type=jnp.float32
+                )
+
+            send1[t, 0:group, :] = base[t, second_rows, :].astype(jnp.bfloat16)
+            send1[t, group:2 * group, :] = base[t, cross_rows, :].astype(jnp.bfloat16)
+            sum_copy1(t).start()
+
+        @pl.when((t >= 2) & (t < PARTS + 2))
+        def _():
+            n = t - 2
+            sum_copy1(n).wait_recv()
+            send2[n] = (
+                base[n, first_rows, :] + recv1[n, group:2 * group, :].astype(jnp.float32)
+            ).astype(jnp.bfloat16)
+            sum_copy2(n).start()
+            base[n, own_rows, :] += recv1[n, 0:group, :].astype(jnp.float32)
+
+        @pl.when((t >= 3) & (t < PARTS + 3))
+        def _():
+            n = t - 3
+            sum_copy2(n).wait_recv()
+            total = base[n, own_rows, :] + recv2[n].astype(jnp.float32)
+            base[n, pl.ds(0, own), :] = total[0:own]
+            for k in range(1, ZS):
+                send3[n, k - 1] = total[k * own:(k + 1) * own].astype(jnp.bfloat16)
+                sum_copy3(n, k).start()
+
+        @pl.when(t >= 4)
+        def _():
+            n = t - 4
+            total = base[n, pl.ds(0, own), :]
+            for k in range(1, ZS):
+                sum_copy3(n, k).wait_recv()
+                total += recv3[n, k - 1].astype(jnp.float32)
+            whole = pl.ds(pl.multiple_of(n * columns, columns), columns)
+            out_ref[:, whole] = total.astype(jnp.bfloat16)
+
+        return carry
+
+    lax.fori_loop(0, PARTS + 4, sum_step, 0)
+
+    @pl.loop(0, STEPS)
+    def _(c):
+        for k in range(1, ZS):
+            z_copy(c, k).wait_send()
+        for copy in near_copies(c):
+            copy.wait_send()
+        cross_copy(c).wait_send()
+
+    @pl.loop(0, tiles)
+    def _(j):
+        core_copy(j).wait_send()
+
+    low_copy.wait_send()
+
+    @pl.loop(0, tiles + 1)
+    def _(j):
+        hidden_copy(j).wait_send()
+
+    @pl.loop(0, PARTS)
+    def _(n):
+        sum_copy1(n).wait_send()
+        sum_copy2(n).wait_send()
+        for k in range(1, ZS):
+            sum_copy3(n, k).wait_send()
+
+
+def fused(
+    tokens,
+    gate_projection_weight,
+    up_projection_weight,
+    down_projection_weight,
+    adapter_down_store,
+    adapter_up_store,
+    request_adapter_index,
+    adapter_store_row,
+):
+    own, features = tokens.shape
+    rows = request_adapter_index.shape[0]
+    units = gate_projection_weight.shape[1]
+    held, rank, _ = adapter_down_store.shape
+    ranks = held * rank
+    width = features // STEPS
+    columns = features // PARTS
+    tiles = units // TILE
+    group = ZS * own
+    bf16, f32 = jnp.bfloat16, jnp.float32
+    dma = pltpu.SemaphoreType.DMA
+    vmem = pl.BlockSpec(memory_space=pltpu.VMEM)
+    hbm = pl.BlockSpec(memory_space=pl.ANY)
+    return pl.pallas_call(
+        layer_kernel,
+        out_shape=jax.ShapeDtypeStruct((own, features), bf16),
+        in_specs=[vmem, hbm, hbm, hbm, hbm, hbm, vmem, vmem],
+        out_specs=vmem,
+        scratch_shapes=[
+            pltpu.VMEM((STEPS, rows, width), bf16),
+            pltpu.VMEM((SLOTS, width, units), bf16),
+            pltpu.VMEM((SLOTS, width, units), bf16),
+            pltpu.VMEM((SLOTS, ranks, width), bf16),
+            pltpu.VMEM((units + ranks, features), bf16),
+            pltpu.VMEM((tiles, rows, 2 * TILE), f32),
+            pltpu.VMEM((rows, ranks), f32),
+            pltpu.VMEM((tiles, rows // 2, 2 * TILE), f32),
+            pltpu.VMEM((rows // 2, ranks), f32),
+            pltpu.VMEM((rows, units + ranks), bf16),
+            pltpu.VMEM((PARTS, rows, columns), f32),
+            pltpu.VMEM((PARTS, 2 * group, columns), bf16),
+            pltpu.VMEM((PARTS, 2 * group, columns), bf16),
+            pltpu.VMEM((PARTS, group, columns), bf16),
+            pltpu.VMEM((PARTS, group, columns), bf16),
+            pltpu.VMEM((PARTS, ZS - 1, own, columns), bf16),
+            pltpu.VMEM((PARTS, ZS - 1, own, columns), bf16),
+            pltpu.VMEM((rows, 1), jnp.int32),
+            dma((3, SLOTS)),
+            dma((2,)),
+            dma((STEPS, ZS - 1)),
+            dma((STEPS, ZS - 1)),
+            dma((3, STEPS)),
+            dma((3, STEPS)),
+            dma((tiles + 1,)),
+            dma((tiles + 1,)),
+            dma((tiles + 1,)),
+            dma((tiles + 1,)),
+            dma((2, PARTS)),
+            dma((2, PARTS)),
+            dma((PARTS, ZS - 1)),
+            dma((PARTS, ZS - 1)),
+        ],
+        compiler_params=pltpu.CompilerParams(
+            collective_id=0, has_side_effects=True, vmem_limit_bytes=61 * 1024 * 1024
+        ),
+    )(
+        tokens,
+        gate_projection_weight,
+        up_projection_weight,
+        down_projection_weight,
+        adapter_down_store.reshape(ranks, features),
+        adapter_up_store.reshape(ranks, features),
+        request_adapter_index.reshape(rows, 1),
+        adapter_store_row.reshape(1, adapter_store_row.shape[0]),
+    )
+
+
 def solution(mesh):
+    small = mesh.shape["tp"] == 16 and mesh.shape["rep"] == 1
     return jax.shard_map(
-        on_device,
+        fused if small else plain,
         mesh=mesh,
         in_specs=(
             P(("rep", "tp"), "sub"),

time: 248 us -> 82.9 us (0.33)
  waiting for transfers between devices: 161 us -> 0 us
  Pallas kernels: 0 us -> 79.7 us
  matrix products: 43.4 us -> 0 us
  between operations: 15.7 us -> 0.01 us
  local copies, waits for them, and re-layouts: 14.7 us -> 3.04 us
  other arithmetic: 8.18 us -> 0 us
  blocking collectives: 3.62 us -> 0 us
    reduce_scatter x1 -> x0, waiting for transfers between devices: 94.4 us -> none  [on_device(): lax.psum_scatter(base_rows + adapter_output, 'tp', scatter_dimension=0, t...]
    pallas_call x0 -> x1, Pallas kernels: none -> 79.7 us  [fused(): pl.pallas_call(layer_kernel, out_shape=jax.ShapeDtypeStruct((own, feature...]
    all_gather x1 -> x0, waiting for transfers between devices: 66.3 us -> none  [on_device(): every_row = lax.all_gather(tokens, 'tp', axis=0, tiled=True)]
    dot_general x11 -> x0, matrix products: 43.4 us -> none  [the longest x1 13.5 us: on_device(): jnp.dot(hidden, down_projection_weight, preferred_element_type=jnp.float32)]
    dynamic_update_slice x4 -> x0, local copies, waits for them, and re-layouts: 11.6 us -> none  [on_device(): lax.dynamic_update_slice_in_dim(adapter_output, current + product, begins...]
    reduce_sum x2 -> x0, other arithmetic: 3.95 us -> none  [the longest x1 3.25 us: on_device(): offset = jnp.sum((request_adapter_index < adapter).astype(jnp.int32))]
    psum x1 -> x0, blocking collectives: 3.62 us -> none  [on_device(): gate_sum, up_sum, low_sum = lax.psum((gate_part, up_part, low_parts), 'sub')]
    eq x1 -> x0, other arithmetic: 2.6 us -> none  [on_device(): lax.dynamic_slice_in_dim(request_adapter_index, row_begin, row_span, 0)]
  transfers between devices with their start and end apart: 3 -> 0, of which waited for: 2 -> 0; matrix products, arithmetic and copies ran while one was open for 12% -> 0% of each run, Pallas kernels for 0% -> 0%
where the time goes in v1:
time: 82.9 us; the launch traced here: 82.7 us
  Pallas kernels  79.7 us (96%)
  local copies, waits for them, and re-layouts  3.04 us (4%)
    pallas_call x1, Pallas kernels, fused(): pl.pallas_call(layer_kernel, out_shape=jax.ShapeDtypeStruct((own, feature...  79.7 us

profile of v1, /device:TPU:0, one launch (start us, length us, event | category | flops | bytes accessed | tf_op | source)
XLA Modules:
  0.0 82.7 jit_solution(16787415145639016300)
XLA Ops:
  0.0 1.5 %copy.9.index_ref = s32[256,1]{1,0:T(8,128)} copy(s32[256,1]{0,1:T(1,128)} %bitcast.6) | data formatting | bytes 2048 | tf_op jit(solution)/shard_map/reshape | solution.py:427
  1.5 79.7 %shard_map.82 = bf16[16,4096]{1,0:T(8,128)(2,1)} custom-call(bf16[16,4096]{1,0:T(8,128)(2,1)} %tokens_ref.1, bf16[4096,1792]{1,0:T(8,128)(2,1)} %gate_hbm.1, bf16[4096,1792]{1,0:T(8,128)(2,1)} %up_hbm.1, bf16[1792,4096]{1,0:T(8,128)(2,1)} %down_hbm.1, bf16[256,4096]{1,0:T(8,128)(2,1)} %bitcast.4, bf16[256,4096]{1,0:T(8,128)(2,1)} %bitcast.5, ...), custom_call_target="tpu_custom_call" | custom-call | tf_op jit(solution)/shard_map/pallas_call | solution.py:378
  81.1 1.6 %copy.11 = bf16[16,4096]{1,0:T(8,128)(2,1)} copy(bf16[16,4096]{1,0:T(8,128)(2,1)} %shard_map.82) | data formatting | bytes 262144

commit v2 on v1

--- a/solution.py
+++ b/solution.py
@@ -7,10 +7,12 @@
 
 MESH = pl.DeviceIdType.MESH
 ZS = 4
-STEPS = 8
-SLOTS = 6
+STEPS = 4
+SLOTS = 3
 PARTS = 8
 TILE = 256
+GATHER_LAGS = (1, 3)
+SUM_LAGS = (2, 4, 6)
 
 
 def plain(
@@ -76,7 +78,7 @@
     tokens_ref, gate_hbm, up_hbm, down_hbm, adown_hbm, aup_hbm, index_ref, store_ref,
     out_ref,
     tok, wg, wu, wa, wd, acc, low, from_core, low_from_core, hid, base,
-    send1, recv1, send2, recv2, send3, recv3, index_rel,
+    send1, recv1, send2, recv2, send3, recv3, index_all, index_rel,
     w_sem, d_sem, z_send, z_recv, n_send, n_recv, e_send, e_recv, h_send, h_recv,
     r_send, r_recv, rz_send, rz_recv,
 ):
@@ -192,10 +194,11 @@
         acc[j] = jnp.zeros(acc.shape[1:], jnp.float32)
 
     low[...] = jnp.zeros_like(low)
+    index_all[...] = jnp.broadcast_to(index_ref[...].astype(jnp.float32), (128, rows)).T
     for q in range(4):
         for k in range(ZS):
             source = pl.ds(pl.multiple_of(place(q, k) * own, own), own)
-            index_rel[pl.ds(q * group + k * own, own), :] = index_ref[source, :]
+            index_rel[pl.ds(q * group + k * own, own), :] = index_all[source, :]
 
     def gather_step(t, carry):
         @pl.when(t < STEPS)
@@ -205,23 +208,22 @@
             for copy in near_copies(t):
                 copy.start()
 
-        @pl.when((t >= 1) & (t < STEPS + 1))
-        def _():
-            near_copies(t - 1)[0].wait_recv()
-            cross_copy(t - 1).start()
-
-        @pl.when(t >= 2)
-        def _():
-            c = t - 2
+        @pl.when((t >= GATHER_LAGS[0]) & (t < STEPS + GATHER_LAGS[0]))
+        def _():
+            near_copies(t - GATHER_LAGS[0])[0].wait_recv()
+            cross_copy(t - GATHER_LAGS[0]).start()
+
+        @pl.when(t >= GATHER_LAGS[1])
+        def _():
+            c = t - GATHER_LAGS[1]
             slot = c % SLOTS
             near_copies(c)[1].wait_recv()
             cross_copy(c).wait_recv()
             for copy in weight_copies(c):
                 copy.wait()
 
-            @pl.loop(0, tiles)
-            def _(j):
-                part = pl.ds(pl.multiple_of(j * TILE, TILE), TILE)
+            for j in range(tiles):
+                part = pl.ds(j * TILE, TILE)
                 acc[j, :, 0:TILE] += jnp.dot(
                     tok[c], wg[slot, :, part], preferred_element_type=jnp.float32
                 )
@@ -244,7 +246,7 @@
 
         return carry
 
-    lax.fori_loop(0, STEPS + 2, gather_step, 0)
+    lax.fori_loop(0, STEPS + GATHER_LAGS[1], gather_step, 0)
     low_copy.start()
 
     @pl.loop(0, tiles)
@@ -260,10 +262,10 @@
     adapters = store_ref.shape[1]
     ranks = low.shape[1]
     local = ranks // 64
-    numbers = lax.broadcasted_iota(jnp.int32, (half, adapters), 1)
+    numbers = lax.broadcasted_iota(jnp.int32, (half, adapters), 1).astype(jnp.float32)
     store = jnp.broadcast_to(store_ref[...].astype(jnp.float32), (half, adapters))
     row_of = jnp.sum(
-        jnp.where(index_rel[my_half, :] == numbers, store, 0.0), axis=1, keepdims=True
+        jnp.where(index_rel[my_half, 0:adapters] == numbers, store, 0.0), axis=1, keepdims=True
     )
     held = lax.broadcasted_iota(jnp.int32, (half, ranks), 1) // 64 + tp * local
     low_sum = low[my_half, :] + low_from_core[...]
@@ -280,9 +282,8 @@
     def sum_step(t, carry):
         @pl.when(t < PARTS)
         def _():
-            @pl.loop(0, columns // TILE)
-            def _(i):
-                part = pl.ds(pl.multiple_of(i * TILE, TILE), TILE)
+            for i in range(columns // TILE):
+                part = pl.ds(i * TILE, TILE)
                 whole = pl.ds(pl.multiple_of(t * columns + i * TILE, TILE), TILE)
                 base[t, :, part] = jnp.dot(
                     hid[...], wd[:, whole], preferred_element_type=jnp.float32
@@ -292,9 +293,9 @@
             send1[t, group:2 * group, :] = base[t, cross_rows, :].astype(jnp.bfloat16)
             sum_copy1(t).start()
 
-        @pl.when((t >= 2) & (t < PARTS + 2))
-        def _():
-            n = t - 2
+        @pl.when((t >= SUM_LAGS[0]) & (t < PARTS + SUM_LAGS[0]))
+        def _():
+            n = t - SUM_LAGS[0]
             sum_copy1(n).wait_recv()
             send2[n] = (
                 base[n, first_rows, :] + recv1[n, group:2 * group, :].astype(jnp.float32)
@@ -302,9 +303,9 @@
             sum_copy2(n).start()
             base[n, own_rows, :] += recv1[n, 0:group, :].astype(jnp.float32)
 
-        @pl.when((t >= 3) & (t < PARTS + 3))
-        def _():
-            n = t - 3
+        @pl.when((t >= SUM_LAGS[1]) & (t < PARTS + SUM_LAGS[1]))
+        def _():
+            n = t - SUM_LAGS[1]
             sum_copy2(n).wait_recv()
             total = base[n, own_rows, :] + recv2[n].astype(jnp.float32)
             base[n, pl.ds(0, own), :] = total[0:own]
@@ -312,9 +313,9 @@
                 send3[n, k - 1] = total[k * own:(k + 1) * own].astype(jnp.bfloat16)
                 sum_copy3(n, k).start()
 
-        @pl.when(t >= 4)
-        def _():
-            n = t - 4
+        @pl.when(t >= SUM_LAGS[2])
+        def _():
+            n = t - SUM_LAGS[2]
             total = base[n, pl.ds(0, own), :]
             for k in range(1, ZS):
                 sum_copy3(n, k).wait_recv()
@@ -324,7 +325,7 @@
 
         return carry
 
-    lax.fori_loop(0, PARTS + 4, sum_step, 0)
+    lax.fori_loop(0, PARTS + SUM_LAGS[2], sum_step, 0)
 
     @pl.loop(0, STEPS)
     def _(c):
@@ -398,7 +399,8 @@
             pltpu.VMEM((PARTS, group, columns), bf16),
             pltpu.VMEM((PARTS, ZS - 1, own, columns), bf16),
             pltpu.VMEM((PARTS, ZS - 1, own, columns), bf16),
-            pltpu.VMEM((rows, 1), jnp.int32),
+            pltpu.VMEM((rows, 128), f32),
+            pltpu.VMEM((rows, 128), f32),
             dma((3, SLOTS)),
             dma((2,)),
             dma((STEPS, ZS - 1)),
@@ -424,7 +426,7 @@
         down_projection_weight,
         adapter_down_store.reshape(ranks, features),
         adapter_up_store.reshape(ranks, features),
-        request_adapter_index.reshape(rows, 1),
+        request_adapter_index.reshape(1, rows),
         adapter_store_row.reshape(1, adapter_store_row.shape[0]),
     )
 

time: 82.9 us -> 72.3 us (0.87)
  Pallas kernels: 79.7 us -> 70.5 us
  local copies, waits for them, and re-layouts: 3.04 us -> 1.57 us
    pallas_call x1, Pallas kernels: 79.7 us -> 70.5 us  [fused(): pl.pallas_call(layer_kernel, out_shape=jax.ShapeDtypeStruct((own, feature...]
    reshape x1 -> x0, local copies, waits for them, and re-layouts: 1.47 us -> none  [fused(): request_adapter_index.reshape(rows, 1)]
where the time goes in v2:
time: 72.3 us; the launch traced here: 72.1 us
  Pallas kernels  70.5 us (98%)
  local copies, waits for them, and re-layouts  1.57 us (2%)
    pallas_call x1, Pallas kernels, fused(): pl.pallas_call(layer_kernel, out_shape=jax.ShapeDtypeStruct((own, feature...  70.5 us
    unnamed x1, local copies, waits for them, and re-layouts  1.57 us

profile of v2, /device:TPU:0, one launch (start us, length us, event | category | flops | bytes accessed | tf_op | source)
XLA Modules:
  0.0 72.1 jit_solution(6117549291823620067)
XLA Ops:
  0.0 70.5 %shard_map.82 = bf16[16,4096]{1,0:T(8,128)(2,1)} custom-call(bf16[16,4096]{1,0:T(8,128)(2,1)} %tokens_ref.1, bf16[4096,1792]{1,0:T(8,128)(2,1)} %gate_hbm.1, bf16[4096,1792]{1,0:T(8,128)(2,1)} %up_hbm.1, bf16[1792,4096]{1,0:T(8,128)(2,1)} %down_hbm.1, bf16[256,4096]{1,0:T(8,128)(2,1)} %bitcast.4, bf16[256,4096]{1,0:T(8,128)(2,1)} %bitcast.5, ...), custom_call_target="tpu_custom_call" | custom-call | tf_op jit(solution)/shard_map/pallas_call | solution.py:379
  70.5 1.6 %copy.10 = bf16[16,4096]{1,0:T(8,128)(2,1)} copy(bf16[16,4096]{1,0:T(8,128)(2,1)} %shard_map.82) | data formatting | bytes 262144
